TPU v7x, 512 devices: a whole 4x4x16 slice. The times are simulated.
512 devices in a mesh: round: 8 (over x, core), brick: 64 (over y, z).
Axes of the slice: x: 4, y: 4, z: 16, core: 2. Of those that a mesh axis runs over, the one named last changes fastest.
Arguments:
- image: bfloat16 [8, 512, 4, 32, 8, 128], P('round', 'brick'), may hold values from -60 to 60
- shifts: int32 [8, 512], P('round', 'brick'), may hold values from -24 to 24, as said below
- fractions: float32 [8, 512], P('round', 'brick'), may hold values from 0 to 1
- valid: int32 [512], replicated, may hold values from 0 to 1, as said below
Outputs:
- spots: bfloat16 [8, 8, 64, 4, 32, 8, 128], P(None, 'round', 'brick')
Inputs may be any that keep to these rules, and one draw needn't show every extreme that they name: `shifts`: in every round, the last brick of each aligned block of 8 bricks has a shift between minus 24 and minus half of 24 (rounded down), and the first brick of each such block a shift between half of 24 (rounded down) and 24. `valid`: the first and the last brick of each aligned block of 8 bricks hold tissue.
All inputs are finite; a program needn't handle non-finite values.
Results may differ from a plain program's by a relative error of at most 0.0055.
Values may be sent and summed in bfloat16 or wider, within the bound.
A program may use at most 128 MiB of HBM per device.

v0:
```python
import functools

import jax
import jax.numpy as jnp
from jax import lax
from jax.sharding import Mesh
from jax.sharding import PartitionSpec as P

SMAX = 24
ROUND = ("round_0", "round_1")
BRICK = ("brick_0", "brick_1")
ROUND_BRICK = ("round_0", "round_1", "brick_0", "brick_1")


sigma_spot = 1.5


def with_halo(cells, sides, width):
    for axis, dim in sides:
        count = lax.axis_size(axis)
        ends = count - 1
        head = lax.slice_in_dim(cells, 0, width, axis=dim)
        tail = lax.slice_in_dim(cells, cells.shape[dim] - width, cells.shape[dim], axis=dim)
        cells = jnp.concatenate(
            [
                lax.ppermute(tail, axis, [(i, (i + 1) % count) for i in range(ends)]),
                cells,
                lax.ppermute(head, axis, [((i + 1) % count, i) for i in range(ends)]),
            ],
            axis=dim,
        )
    return cells


def by_axis(shard, axes):
    return functools.reduce(lax.psum, axes, shard)


def kernel_tables(count):
    index = jnp.arange(count, dtype=jnp.float32)
    offset = index[:, None] - index[None, :]
    smooth = jnp.exp(-offset * offset / (2.0 * sigma_spot * sigma_spot)) / (
        2.5066282746310002 * sigma_spot
    )
    smooth = jnp.where(jnp.abs(offset) < 4.0 * sigma_spot, smooth, jnp.float32(0.0))
    curve = (offset * offset / sigma_spot**4 - 1.0 / sigma_spot**2) * smooth
    return (smooth, curve)


def spot_filter(field):
    values = field.astype(jnp.float32)
    depth, height, width = field.shape[-3:]
    gauss_z, curve_z = kernel_tables(depth)
    gauss_y, curve_y = kernel_tables(height)
    gauss_x, curve_x = kernel_tables(width)
    high = lax.Precision.HIGHEST
    along_x = jnp.einsum("...x,wx->...w", values, gauss_x, precision=high)
    bent_x = jnp.einsum("...x,wx->...w", values, curve_x, precision=high)
    plain_y = jnp.einsum("...yx,vy->...vx", along_x, gauss_y, precision=high)
    bent_y = jnp.einsum("...yx,vy->...vx", along_x, curve_y, precision=high)
    mixed_y = jnp.einsum("...yx,vy->...vx", bent_x, gauss_y, precision=high)
    outer = jnp.einsum("...zyx,wz->...wyx", mixed_y + bent_y, gauss_z, precision=high)
    outer = outer + jnp.einsum("...zyx,wz->...wyx", plain_y, curve_z, precision=high)
    return (-(sigma_spot * sigma_spot) * outer).astype(jnp.bfloat16)


def on_device(image, shifts, fractions, valid):
    layer = image[0]
    bricks_here, channels, depth, height, width = layer.shape
    rounds = lax.axis_size(ROUND)
    brick_index = lax.axis_index(BRICK)
    round_index = lax.axis_index(ROUND)
    reach = SMAX + 1
    own_valid = lax.dynamic_slice_in_dim(valid, brick_index * bricks_here, bricks_here)
    masked = layer * own_valid.astype(jnp.bfloat16)[:, None, None, None, None]
    strip = jnp.moveaxis(masked, 0, 3).reshape(channels, depth, height, bricks_here * width)
    padded = with_halo(strip, ((BRICK, 3),), reach)
    offsets = jnp.arange(bricks_here, dtype=jnp.int32) * width + reach - shifts[0] - 1

    def one_brick(start, fraction):
        window = lax.dynamic_slice_in_dim(padded, start, width + 1, 3).astype(jnp.float32)
        return ((1.0 - fraction) * window[..., 1:] + fraction * window[..., :-1]).astype(
            jnp.bfloat16
        )

    shifted = jax.vmap(one_brick)(offsets, fractions[0])
    filtered = spot_filter(shifted)
    magnitude = jnp.sum(jnp.abs(filtered.astype(jnp.float32)), axis=(2, 3, 4))
    sums = jnp.sum(magnitude * own_valid.astype(jnp.float32)[:, None], axis=0)
    selector = (jnp.arange(rounds, dtype=jnp.int32) == round_index).astype(jnp.float32)
    stats = selector[:, None] * sums[None, :]
    moved = lax.all_to_all(filtered[None], ROUND, split_axis=1, concat_axis=0, tiled=True)
    totals = by_axis(stats, ROUND_BRICK)
    count = jnp.maximum(jnp.sum(valid).astype(jnp.float32), 1.0)
    scale = totals / (count * depth * height * width) + 1e-06
    ratio = moved.astype(jnp.float32) / scale[:, None, :, None, None, None]
    energy = jnp.mean(ratio * ratio, axis=(0, 2), keepdims=True)
    normed = (ratio / jnp.sqrt(energy + 1.0)).astype(jnp.bfloat16)
    return normed[:, None]


def solution(mesh):
    split = Mesh(mesh.devices.reshape(4, 2, 4, 16), ("round_0", "round_1", "brick_0", "brick_1"))
    return jax.shard_map(
        on_device,
        mesh=split,
        in_specs=(P(ROUND, BRICK, None, None, None, None), P(ROUND, BRICK), P(ROUND, BRICK), P()),
        out_specs=P(None, ROUND, BRICK, None, None, None, None),
        check_vma=False,
    )
```

profile of v0, /device:TPU:8, one launch (start us, length us, event | category | flops | bytes accessed | tf_op | source)
XLA Modules:
  0.0 173.5 jit_solution(15847041595889608548)
XLA Ops:
  0.0 0.0 copy-start.2
  0.0 0.0 copy-start.1
  0.0 0.8 dynamic-slice_convert_fusion
  0.8 2.3 %copy_bitcast_fusion = bf16[4,32,8,1024]{3,2,1,0:T(8,128)(2,1)S(1)} fusion(bf16[1,8,4,32,8,128]{5,4,3,2,1,0:T(8,128)(2,1)} %param.4, bf16[8]{0:T(256)(128)(2,1)S(1)} %get-tuple-element.8), kind=kLoop, calls=%fused_computation.22 | loop fusion | flops 1048576 | bytes 4194320 | tf_op jit(solution)/shard_map/reshape | solution.py:76
  3.1 0.2 fusion.124
  3.2 3.8 %collective-permute-start = (bf16[4,32,8,25]{3,2,1,0:T(8,128)(2,1)S(1)}, bf16[4,32,8,25]{3,2,1,0:T(8,128)(2,1)S(1)}, u32[]{:S(2)}, u32[]{:S(2)}) collective-permute-start(bf16[4,32,8,25]{3,2,1,0:T(8,128)(2,1)S(1)} %get-tuple-element.6), channel_id=1, source_target_pairs={{0,1},{1,2},{2,3},{3,4},{4,5},{5,6},{6,7},{7,8},{8,9},{9,10},{10,1... | collective-permute-start | bytes 153608 | tf_op jit(solution)/shard_map/ppermute | solution.py:26
  7.1 9.4 %collective-permute-start.1 = (bf16[4,32,8,25]{3,2,1,0:T(8,128)(2,1)S(1)}, bf16[4,32,8,25]{3,2,1,0:T(8,128)(2,1)S(1)}, u32[]{:S(2)}, u32[]{:S(2)}) collective-permute-start(bf16[4,32,8,25]{3,2,1,0:T(8,128)(2,1)S(1)} %get-tuple-element.5), channel_id=1, source_target_pairs={{1,0},{2,1},{3,2},{4,3},{5,4},{6,5},{7,6},{8,7},{9,8},{10,9},{11,1... | collective-permute-start | bytes 153608 | tf_op jit(solution)/shard_map/ppermute | solution.py:28
  16.5 0.0 copy-done.2
  16.5 0.0 copy-done.1
  16.5 4.3 %collective-permute-done = bf16[4,32,8,25]{3,2,1,0:T(8,128)(2,1)S(1)} collective-permute-done((bf16[4,32,8,25]{3,2,1,0:T(8,128)(2,1)S(1)}, bf16[4,32,8,25]{3,2,1,0:T(8,128)(2,1)S(1)}, u32[]{:S(2)}, u32[]{:S(2)}) %collective-permute-start) | collective-permute-done | bytes 51232 | tf_op jit(solution)/shard_map/ppermute | solution.py:26
  20.8 1.2 collective-permute-done.1
  22.0 4.0 %concatenate.6 = bf16[4,32,8,1074]{3,2,1,0:T(8,128)(2,1)} concatenate(bf16[4,32,8,25]{3,2,1,0:T(8,128)(2,1)S(1)} %collective-permute-done, bf16[4,32,8,1024]{3,2,1,0:T(8,128)(2,1)S(1)} %copy_bitcast_fusion, bf16[4,32,8,25]{3,2,1,0:T(8,128)(2,1)S(1)} %collective-permute-done.1), dimensions={3} | concatenate | bytes 4399104 | tf_op jit(solution)/shard_map/concatenate | solution.py:24
  26.0 16.7 %copy.31 = bf16[4,32,8,1074]{1,2,0,3:T(8,128)(2,1)} copy(bf16[4,32,8,1074]{3,2,1,0:T(8,128)(2,1)} %concatenate.6) | data formatting | bytes 4399104 | tf_op jit(solution)/shard_map/concatenate | solution.py:24
  42.7 8.3 %gather_fusion = bf16[8,4,32,8,129]{2,3,1,4,0:T(8,128)(2,1)} fusion(bf16[4,32,8,1074]{1,2,0,3:T(8,128)(2,1)} %copy.31, s32[8]{0:T(128)S(1)} %shift-left_bitcast_fusion), kind=kCustom, calls=%fused_computation | custom fusion | bytes 4227200 | tf_op jit(solution)/shard_map/vmap()/gather | solution.py:81
  51.0 13.0 %copy.32 = bf16[8,4,32,8,129]{4,3,2,1,0:T(8,128)(2,1)} copy(bf16[8,4,32,8,129]{2,3,1,4,0:T(8,128)(2,1)} %gather_fusion) | data formatting | bytes 4227072 | tf_op jit(solution)/shard_map/vmap()/gather | solution.py:81
  64.0 3.2 %convert_element_type.72 = f32[8,4,32,8,129]{4,3,2,1,0:T(8,128)S(1)} convert(bf16[8,4,32,8,129]{4,3,2,1,0:T(8,128)(2,1)} %copy.32) | non-fusion elementwise | flops 1056768 | bytes 6340608 | tf_op jit(solution)/shard_map/vmap()/convert_element_type | solution.py:81
  67.2 1.5 fusion.5
  68.7 1.8 %fusion.18 = f32[8,4,32,8,128]{4,3,2,1,0:T(8,128)S(1)} fusion(bf16[8,4,32,8,128]{4,3,2,1,0:T(8,128)(2,1)S(1)} %fusion.5), kind=kOutput, calls=%fused_computation.29 | convolution fusion | flops 1610743808 | bytes 6291456 | tf_op jit(solution)/shard_map/...x,wx->...w/dot_general | solution.py:57
  70.6 1.8 %fusion.20 = f32[8,4,32,8,128]{4,3,2,1,0:T(8,128)S(1)} fusion(bf16[8,4,32,8,128]{4,3,2,1,0:T(8,128)(2,1)S(1)} %fusion.5), kind=kOutput, calls=%fused_computation.31 | convolution fusion | flops 1610809344 | bytes 6291456 | tf_op jit(solution)/shard_map/...x,wx->...w/dot_general | solution.py:58
  72.4 3.6 %fusion.66 = f32[8,8,4,32,128]{4,0,3,2,1:T(8,128)S(1)} fusion(f32[8,4,32,8,128]{4,3,2,1,0:T(8,128)S(1)} %fusion.20), kind=kOutput, calls=%fused_computation.79 | convolution fusion | flops 100663808 | bytes 8388608 | tf_op jit(solution)/shard_map/...yx,vy->...vx/dot_general | solution.py:61
  76.0 3.9 %convolution_bitcast_fusion = f32[8,4,32,8,128]{4,3,2,1,0:T(8,128)S(1)} fusion(f32[8,4,32,8,128]{4,3,2,1,0:T(8,128)S(1)} %fusion.18), kind=kOutput, calls=%fused_computation.19 | convolution fusion | flops 100663808 | bytes 8388608 | tf_op jit(solution)/shard_map/...yx,vy->...vx/dot_general | solution.py:59
  79.9 3.6 %add_bitcast_fusion = f32[8,4,32,8,128]{4,3,2,1,0:T(8,128)S(1)} fusion(f32[8,8,4,32,128]{4,0,3,2,1:T(8,128)S(1)} %fusion.66, f32[8,4,32,8,128]{4,3,2,1,0:T(8,128)S(1)} %fusion.18), kind=kOutput, calls=%fused_computation.17 | convolution fusion | flops 101712640 | bytes 12582912 | tf_op jit(solution)/shard_map/...yx,vy->...vx/dot_general | solution.py:60
  83.6 3.8 %fusion.6 = f32[32,8,4,8,128]{4,0,3,2,1:T(8,128)S(1)} fusion(f32[8,4,32,8,128]{4,3,2,1,0:T(8,128)S(1)} %convolution_bitcast_fusion), kind=kOutput, calls=%fused_computation.11 | convolution fusion | flops 402665472 | bytes 8388608 | tf_op jit(solution)/shard_map/...zyx,wz->...wyx/dot_general | solution.py:63
  87.4 5.3 %abs_reduce_fusion = (f32[8,4]{1,0:T(8,128)S(1)}, bf16[32,8,4,8,128]{4,0,3,2,1:T(8,128)(2,1)}) fusion(f32[32,8,4,8,128]{4,0,3,2,1:T(8,128)S(1)} %fusion.6, f32[8,4,32,8,128]{4,3,2,1,0:T(8,128)S(1)} %add_bitcast_fusion), kind=kOutput, calls=%fused_computation.15 | convolution fusion | flops 408952800 | bytes 10485888 | tf_op jit(solution)/shard_map/...zyx,wz->...wyx/dot_general | solution.py:62
  92.7 0.0 copy-start
  92.7 4.4 %all-to-all-start = ((bf16[1,8,4,32,8,128]{5,3,4,2,0,1:T(8,128)(2,1)}), bf16[1,8,4,32,8,128]{5,3,4,2,0,1:T(8,128)(2,1)S(1)}, u32[]{:S(2)}, u32[]{:S(2)}) async-start(bf16[1,8,4,32,8,128]{5,3,4,2,0,1:T(8,128)(2,1)} %bitcast.83), calls=%async_computation | async-start | bytes 4194304 | tf_op jit(solution)/shard_map/all_to_all | solution.py:92
  97.1 0.0 copy-done
  97.1 0.7 reduce_sum.38
  98.5 0.1 multiply_reduce_fusion
  98.6 0.1 broadcast_multiply_fusion
  98.7 27.9 %psum.28 = f32[8,4]{1,0:T(8,128)S(1)} all-reduce(f32[8,4]{1,0:T(8,128)S(1)} %broadcast_multiply_fusion), channel_id=1, replica_groups=mesh['round_0'=4,'round_1'=2,'brick_0'=4,'brick_1'=16] {'round_0'}, use_global_device_ids=true, to_apply=%region_2.3 | all-reduce | flops 32 | bytes 256 | tf_op jit(solution)/shard_map/psum | solution.py:36
  126.6 2.5 %psum.29 = f32[8,4]{1,0:T(8,128)S(1)} all-reduce(f32[8,4]{1,0:T(8,128)S(1)} %psum.28), channel_id=1, replica_groups=mesh['round_0'=4,'round_1'=2,'brick_0'=4,'brick_1'=16] {'round_1'}, use_global_device_ids=true, to_apply=%region_3.4 | all-reduce | flops 32 | bytes 256 | tf_op jit(solution)/shard_map/psum | solution.py:36
  129.0 8.7 %psum.30 = f32[8,4]{1,0:T(8,128)S(1)} all-reduce(f32[8,4]{1,0:T(8,128)S(1)} %psum.29), channel_id=1, replica_groups=mesh['round_0'=4,'round_1'=2,'brick_0'=4,'brick_1'=16] {'brick_0'}, use_global_device_ids=true, to_apply=%region_4.5 | all-reduce | flops 32 | bytes 256 | tf_op jit(solution)/shard_map/psum | solution.py:36
  137.7 32.0 %psum.31 = f32[8,4]{1,0:T(8,128)S(1)} all-reduce(f32[8,4]{1,0:T(8,128)S(1)} %psum.30), channel_id=1, replica_groups=mesh['round_0'=4,'round_1'=2,'brick_0'=4,'brick_1'=16] {'brick_1'}, use_global_device_ids=true, to_apply=%region_5.6 | all-reduce | flops 32 | bytes 256 | tf_op jit(solution)/shard_map/psum | solution.py:36
  169.7 0.0 all-to-all-done
  169.7 0.6 fusion.10
  170.4 0.8 fusion.1
  171.2 2.3 %copy.37 = bf16[8,1,1,4,32,8,128]{6,5,4,3,2,1,0:T(8,128)(2,1)} copy(bf16[8,1,1,4,32,8,128]{6,4,5,3,0,2,1:T(8,128)(2,1)S(1)} %fusion.1) | data formatting | bytes 4194304 | tf_op jit(solution)/shard_map/convert_element_type | solution.py:98
  (5 shorter events, 0.1 us)
Async XLA Ops:
  0.0 16.5 %copy-start.2 = (s32[1,8]{1,0:T(1,128)S(1)}, s32[1,8]{1,0:T(1,128)}, u32[]{:S(2)}) copy-start(s32[1,8]{1,0:T(1,128)} %param.5) | copy-start | bytes 100
  0.0 16.5 %copy-start.1 = (f32[1,8]{1,0:T(1,128)S(1)}, f32[1,8]{1,0:T(1,128)}, u32[]{:S(2)}) copy-start(f32[1,8]{1,0:T(1,128)} %param.6) | copy-start | bytes 100
  3.2 17.6 %collective-permute-start = (bf16[4,32,8,25]{3,2,1,0:T(8,128)(2,1)S(1)}, bf16[4,32,8,25]{3,2,1,0:T(8,128)(2,1)S(1)}, u32[]{:S(2)}, u32[]{:S(2)}) collective-permute-start(bf16[4,32,8,25]{3,2,1,0:T(8,128)(2,1)S(1)} %get-tuple-element.6), channel_id=1, source_target_pairs={{0,1},{1,2},{2,3},{3,4},{4,5},{5,6},{6,7},{7,8},{8,9},{9,10},{10,1... | collective-permute-start | bytes 153608 | tf_op jit(solution)/shard_map/ppermute | solution.py:26
  7.1 14.9 %collective-permute-start.1 = (bf16[4,32,8,25]{3,2,1,0:T(8,128)(2,1)S(1)}, bf16[4,32,8,25]{3,2,1,0:T(8,128)(2,1)S(1)}, u32[]{:S(2)}, u32[]{:S(2)}) collective-permute-start(bf16[4,32,8,25]{3,2,1,0:T(8,128)(2,1)S(1)} %get-tuple-element.5), channel_id=1, source_target_pairs={{1,0},{2,1},{3,2},{4,3},{5,4},{6,5},{7,6},{8,7},{9,8},{10,9},{11,1... | collective-permute-start | bytes 153608 | tf_op jit(solution)/shard_map/ppermute | solution.py:28
  92.7 4.4 %copy-start = (s32[512]{0:T(512)S(1)}, s32[512]{0:T(512)}, u32[]{:S(2)}) copy-start(s32[512]{0:T(512)} %param.7) | copy-start | bytes 6148
  92.7 77.0 %all-to-all-start = ((bf16[1,8,4,32,8,128]{5,3,4,2,0,1:T(8,128)(2,1)}), bf16[1,8,4,32,8,128]{5,3,4,2,0,1:T(8,128)(2,1)S(1)}, u32[]{:S(2)}, u32[]{:S(2)}) async-start(bf16[1,8,4,32,8,128]{5,3,4,2,0,1:T(8,128)(2,1)} %bitcast.83), calls=%async_computation | async-start | bytes 4194304 | tf_op jit(solution)/shard_map/all_to_all | solution.py:92
where the time goes:
time: 174 us; the launch traced here: 173 us
  blocking collectives  71 us (41%)
  local copies, waits for them, and re-layouts  44.4 us (26%)
  matrix products  23.9 us (14%)
  starting transfers between devices  17.6 us (10%)
  other arithmetic  10.2 us (6%)
  waiting for transfers between devices  5.5 us (3%)
    psum x4, blocking collectives, by_axis(): return functools.reduce(lax.psum, axes, shard)  71 us
    gather x2, local copies, waits for them, and re-layouts, one_brick(): lax.dynamic_slice_in_dim(padded, start, width + 1, 3).astype(jnp.float32)  21.2 us
    concatenate x2, local copies, waits for them, and re-layouts, with_halo(): jnp.concatenate([lax.ppermute(tail, axis, [(i, (i + 1) % count) for i in...  20.7 us
    ppermute x1, starting transfers between devices, with_halo(): lax.ppermute(head, axis, [((i + 1) % count, i) for i in range(ends)])  9.38 us
    dot_general x1, matrix products, spot_filter(): jnp.einsum('...zyx,wz->...wyx', mixed_y + bent_y, gauss_z, precision=high)  5.29 us
    all_to_all x1, starting transfers between devices, on_device(): lax.all_to_all(filtered[None], ROUND, split_axis=1, concat_axis=0, tiled=...  4.43 us
    ppermute x1, waiting for transfers between devices, with_halo(): lax.ppermute(tail, axis, [(i, (i + 1) % count) for i in range(ends)])  4.31 us
    dot_general x1, matrix products, spot_filter(): plain_y = jnp.einsum('...yx,vy->...vx', along_x, gauss_y, precision=high)  3.87 us
  transfers between devices with their start and end apart: 3, of which 2 were waited for; matrix products, arithmetic and copies ran while one was open for 1% of the time, Pallas kernels for 0%

commit v1 on v0

v1 whole, which is shorter than its diff:
```python
import functools
import math

import jax
import jax.numpy as jnp
import ml_dtypes
import numpy as np
from jax import lax
from jax.experimental import pallas as pl
from jax.experimental.pallas import tpu as pltpu
from jax.sharding import PartitionSpec as P

MESH = pl.DeviceIdType.MESH
SIGMA = 1.5
HALO = 32
BF16 = jnp.bfloat16
F32 = jnp.float32


def tables(count):
    index = np.arange(count, dtype=np.float64)
    offset = index[:, None] - index[None, :]
    smooth = np.exp(-offset * offset / (2.0 * SIGMA * SIGMA)) / (math.sqrt(2.0 * math.pi) * SIGMA)
    smooth = np.where(np.abs(offset) < 4.0 * SIGMA, smooth, 0.0)
    curve = (offset * offset / SIGMA**4 - 1.0 / SIGMA**2) * smooth
    return smooth, curve


def split(matrix):
    high = matrix.astype(ml_dtypes.bfloat16)
    low = (matrix - high.astype(np.float64)).astype(ml_dtypes.bfloat16)
    return high, low


def weights(depth, height, width):
    gz, sz = tables(depth)
    gy, sy = tables(height)
    gx, sx = tables(width)
    plain = np.kron(gz, gy)
    bent = np.kron(gz, sy) + np.kron(sz, gy)
    zy = -(SIGMA * SIGMA) * np.concatenate([plain, bent], axis=0)
    zy = np.concatenate(split(zy), axis=0)
    x = np.concatenate(split(np.concatenate([sx.T, gx.T], axis=0)), axis=1)
    return zy, x


def iota(shape, dim):
    return lax.broadcasted_iota(jnp.int32, shape, dim)


def dot(a, b):
    return jnp.dot(a, b, preferred_element_type=F32)


def kernel(sizes, img, shifts, fractions, valid, counts, w1h, w2h, out, ext, send, recv, halo_out, halo_in,
           w1, w2, diff, shifted, yhi, ylo, acc, tile_a, tile_b, tile_c, recv_a, recv_b, recv_c, inv,
           load_sem, w_sem, send_sem, recv_sem, halo_ssem, halo_rsem, red_ssem, red_rsem):
    rounds, bricks, zs, ys, voxels = sizes
    channels, area, width = ext.shape[1:]
    me = lax.axis_index("round")
    col = lax.axis_index("brick")
    z = lax.rem(col, zs)
    y = col // zs

    def z_peer(d):
        return y * zs + lax.rem(z + d, zs)

    def y_peer(d):
        return lax.rem(y + d, ys) * zs + z

    last = lax.axis_size("brick")
    right, left = lax.rem(col + 1, last), lax.rem(col + last - 1, last)

    barrier = pltpu.get_barrier_semaphore()
    for d in range(1, rounds):
        pl.semaphore_signal(barrier, inc=1, device_id={"round": lax.rem(me + d, rounds)}, device_id_type=MESH)
    for j in [right, left] + [z_peer(d) for d in range(1, zs)] + [y_peer(d) for d in range(1, ys)]:
        pl.semaphore_signal(barrier, inc=1, device_id={"brick": j}, device_id_type=MESH)

    loads = [pltpu.make_async_copy(img.at[k], ext.at[k + 1], load_sem.at[k]) for k in range(bricks)]
    loads += [pltpu.make_async_copy(w1h, w1, w_sem.at[0]), pltpu.make_async_copy(w2h, w2, w_sem.at[1])]
    for c in loads:
        c.start()

    shape = (width, 2 * width)
    lane = iota(shape, 1)
    diff[...] = iota(shape, 0) - (lane & (width - 1)) + (lane >> 7)
    acc[...] = jnp.zeros_like(acc)
    for c in loads:
        c.wait()

    def pack_mask(shape, packed, long, start):
        p, q = iota(shape, packed), iota(shape, long)
        return jnp.where((p >> 5) * width + start + (p & (HALO - 1)) == q, 1.0, 0.0).astype(BF16)

    def flat(k):
        return jnp.concatenate([ext[k, c] for c in range(channels)], axis=1)

    halo_out[0] = dot(flat(bricks), pack_mask((channels * width, width), 1, 0, width - HALO)).astype(BF16)
    halo_out[1] = dot(flat(1), pack_mask((channels * width, width), 1, 0, 0)).astype(BF16)
    pl.semaphore_wait(barrier, rounds - 1 + 2 + zs - 1 + ys - 1)

    halos = [
        pltpu.make_async_remote_copy(
            src_ref=halo_out.at[i], dst_ref=halo_in.at[i], send_sem=halo_ssem.at[i], recv_sem=halo_rsem.at[i],
            device_id={"brick": j}, device_id_type=MESH)
        for i, j in ((0, right), (1, left))
    ]
    for c in halos:
        c.start()

    def unpack_halos():
        for i, (slot, start) in enumerate(((0, width - HALO), (bricks + 1, 0))):
            halos[i].wait_recv()
            wide = dot(halo_in[i], pack_mask((width, channels * width), 0, 1, start)).astype(BF16)
            for c in range(channels):
                ext[slot, c] = wide[:, c * width:(c + 1) * width]

    chip, core = me // 2, lax.rem(me, 2)
    chips = rounds // 2

    def brick_of(step):
        turn = lax.rem(step, 3)
        late = step // 3
        ahead = jnp.where(turn == 2, 2, jnp.where(turn == core, 1, chips - 1))
        there = lax.rem(chip + ahead, chips)
        first = jnp.where(there < chips // 2, 1, 0)
        far = 2 * there + jnp.where(late == 0, first, 1 - first)
        return jnp.where(step < 6, far, jnp.where(step == 6, 2 * chip + 1 - core, me))

    def bulk(k):
        return pltpu.make_async_remote_copy(
            src_ref=send.at[k], dst_ref=recv.at[me], send_sem=send_sem.at[k], recv_sem=recv_sem.at[me],
            device_id={"round": k}, device_id_type=MESH)

    def filter_brick(k):
        s = shifts[0, k]
        f = fractions[0, k]
        here = col * bricks + k
        v_left = jnp.where(here > 0, valid[jnp.maximum(here - 1, 0)], 0)
        v_right = jnp.where(here < last * bricks - 1, valid[jnp.minimum(here + 1, last * bricks - 1)], 0)
        v_here = valid[here].astype(F32)
        v_next = jnp.where(s >= 0, v_left, v_right).astype(F32)
        t_next = jnp.where(s >= 0, width, -width) - s
        pick = jnp.concatenate([
            jnp.where(diff[...] == -s, v_here, 0.0).astype(BF16),
            jnp.where(diff[...] == t_next, v_next, 0.0).astype(BF16)], axis=0)
        flat_rows = (channels * area, width)
        is_left = jnp.where(s >= 0, 1.0, 0.0).astype(BF16)
        is_right = jnp.where(s >= 0, 0.0, 1.0).astype(BF16)
        beside = ext[k].reshape(flat_rows) * is_left + ext[k + 2].reshape(flat_rows) * is_right
        moved = dot(jnp.concatenate([ext[k + 1].reshape(flat_rows), beside], axis=1), pick)
        shifted[...] = ((1.0 - f) * moved[:, :width] + f * moved[:, width:]).astype(BF16)
        field = jnp.concatenate([shifted[c * area:(c + 1) * area] for c in range(channels)], axis=1)
        planes = dot(w1[:2 * area], field) + dot(w1[2 * area:], field)
        for c in range(channels):
            both = jnp.concatenate([
                planes[:area, c * width:(c + 1) * width], planes[area:, c * width:(c + 1) * width]], axis=1)
            high = both.astype(BF16)
            yhi[c * area:(c + 1) * area] = high
            ylo[c * area:(c + 1) * area] = (both - high.astype(F32)).astype(BF16)
        twice = dot(yhi[...], w2[...])
        result = (twice[:, :width] + twice[:, width:] + dot(ylo[...], w2[:, :width])).astype(BF16)
        send[k] = result.reshape(channels, area, width)
        size = jnp.abs(result.astype(F32)).reshape(channels, area // 8, 8, width)
        acc[...] += jnp.sum(size, axis=1) * v_here

    def step_body(step, _):
        @pl.when(step == 3)
        def _():
            unpack_halos()

        k = brick_of(step)
        filter_brick(k)

        @pl.when(step < rounds - 1)
        def _():
            bulk(k).start()

        return 0

    lax.fori_loop(0, rounds, step_body, 0)
    recv[me] = send[me]

    def gather(tile, slots, peers, index):
        copies = [
            pltpu.make_async_remote_copy(
                src_ref=tile, dst_ref=slots.at[d], send_sem=red_ssem.at[index], recv_sem=red_rsem.at[index],
                device_id=peer, device_id_type=MESH)
            for d, peer in enumerate(peers)
        ]
        for c in copies:
            c.start()
        pltpu.make_async_copy(slots, slots, red_rsem.at[index]).wait()
        return tile[...] + jnp.sum(slots[...], axis=0)

    tile_a[...] = jnp.zeros_like(tile_a)
    tile_a[:channels] = jnp.sum(acc[...], axis=1)
    tile_b[...] = gather(tile_a, recv_a, [{"brick": z_peer(d)} for d in range(1, zs)], 0)
    tile_c[...] = gather(tile_b, recv_b, [{"brick": y_peer(d)} for d in range(1, ys)], 1)
    totals = [
        pltpu.make_async_remote_copy(
            src_ref=tile_c, dst_ref=recv_c.at[me], send_sem=red_ssem.at[2], recv_sem=red_rsem.at[2],
            device_id={"round": lax.rem(me + d, rounds)}, device_id_type=MESH)
        for d in range(1, rounds)
    ]
    for c in totals:
        c.start()
    seven = recv_c.at[pl.ds(0, rounds - 1)]
    pltpu.make_async_copy(seven, seven, red_rsem.at[2]).wait()
    recv_c[me] = tile_c[...]
    count = jnp.maximum(jnp.sum(counts[...].astype(F32)), 1.0)
    total = jnp.sum(recv_c[...], axis=2, keepdims=True)
    inv[...] = jnp.broadcast_to(1.0 / (total / (count * voxels) + 1e-06), inv.shape)

    for d in range(1, rounds):
        source = lax.rem(me + d, rounds)
        pltpu.make_async_copy(recv.at[source], recv.at[source], recv_sem.at[source]).wait()

    def norm_body(i, _):
        rows = pl.ds(pl.multiple_of(i * 16, 16), 16)
        energy = jnp.zeros((16, width), F32)
        for r in range(rounds):
            for c in range(channels):
                a = recv[r, c, rows].astype(F32) * inv[r, c:c + 1]
                energy += a * a
        root = lax.rsqrt(energy * (1.0 / (rounds * channels)) + 1.0)
        for r in range(rounds):
            for c in range(channels):
                a = recv[r, c, rows].astype(F32) * inv[r, c:c + 1]
                out[r, c, rows] = (a * root).astype(BF16)
        return 0

    lax.fori_loop(0, area // 16, norm_body, 0)

    for c in halos:
        c.wait_send()
    for d in range(1, rounds):
        k = lax.rem(me + d, rounds)
        bulk(k).wait_send()
    pltpu.make_async_copy(recv_a, recv_a, red_ssem.at[0]).wait()
    pltpu.make_async_copy(recv_b, recv_b, red_ssem.at[1]).wait()
    pltpu.make_async_copy(seven, seven, red_ssem.at[2]).wait()


def on_device(image, shifts, fractions, valid):
    _, bricks, channels, depth, height, width = image.shape
    rounds = lax.axis_size("round")
    zs, ys = 16, 4
    area = depth * height
    w1, w2 = weights(depth, height, width)
    anywhere = pl.BlockSpec(memory_space=pl.ANY)
    scalars = pl.BlockSpec(memory_space=pltpu.SMEM)
    vector = pl.BlockSpec(memory_space=pltpu.VMEM)
    tile = (8, width)
    sems = pltpu.SemaphoreType.DMA
    out = pl.pallas_call(
        functools.partial(kernel, (rounds, bricks, zs, ys, depth * height * width)),
        out_shape=jax.ShapeDtypeStruct((rounds, channels, area, width), BF16),
        in_specs=[anywhere, scalars, scalars, scalars, vector, anywhere, anywhere],
        out_specs=vector,
        scratch_shapes=[
            pltpu.VMEM((bricks + 2, channels, area, width), BF16),
            pltpu.VMEM((bricks, channels, area, width), BF16),
            pltpu.VMEM((rounds, channels, area, width), BF16),
            pltpu.VMEM((2, area, width), BF16),
            pltpu.VMEM((2, area, width), BF16),
            pltpu.VMEM(w1.shape, BF16),
            pltpu.VMEM(w2.shape, BF16),
            pltpu.VMEM((width, 2 * width), jnp.int32),
            pltpu.VMEM((channels * area, width), BF16),
            pltpu.VMEM((channels * area, 2 * width), BF16),
            pltpu.VMEM((channels * area, 2 * width), BF16),
            pltpu.VMEM((channels,) + tile, F32),
            pltpu.VMEM(tile, F32),
            pltpu.VMEM(tile, F32),
            pltpu.VMEM(tile, F32),
            pltpu.VMEM((zs - 1,) + tile, F32),
            pltpu.VMEM((ys - 1,) + tile, F32),
            pltpu.VMEM((rounds,) + tile, F32),
            pltpu.VMEM((rounds,) + tile, F32),
            sems((bricks,)), sems((2,)), sems((bricks,)), sems((rounds,)), sems((2,)), sems((2,)), sems((3,)),
            sems((3,)),
        ],
        compiler_params=pltpu.CompilerParams(
            collective_id=0, has_side_effects=True, vmem_limit_bytes=48 * 2**20),
        name="spots",
    )(image.reshape(bricks, channels, area, width), shifts, fractions, valid, valid.reshape(-1, width),
      jnp.asarray(w1), jnp.asarray(w2))
    return out.reshape(rounds, 1, 1, channels, depth, height, width)


def solution(mesh):
    return jax.shard_map(
        on_device,
        mesh=mesh,
        in_specs=(P("round", "brick"), P("round", "brick"), P("round", "brick"), P()),
        out_specs=P(None, "round", "brick"),
        check_vma=False,
    )
```

time: 174 us -> 54 us (0.31)
  the two profiles are of different devices: /device:TPU:8 before, /device:TPU:1 now
where the time goes in v1:
time: 54 us; the launch traced here: 53.7 us
  Pallas kernels  46.9 us (87%)
  local copies, waits for them, and re-layouts  6.85 us (13%)
    pallas_call x1, Pallas kernels, on_device(): pl.pallas_call(functools.partial(kernel, (rounds, bricks, zs, ys, depth *...  46.9 us
    unnamed x13, local copies, waits for them, and re-layouts  6.85 us

profile of v1, /device:TPU:1, one launch (start us, length us, event | category | flops | bytes accessed | tf_op | source)
XLA Modules:
  0.0 53.7 jit_solution(15731327614370924165)
XLA Ops:
  0.0 0.0 copy-start
  0.0 1.6 %copy-done = bf16[1,8,4,32,8,128]{5,4,3,2,1,0:T(8,128)(2,1)S(1)} copy-done((bf16[1,8,4,32,8,128]{5,4,3,2,1,0:T(8,128)(2,1)S(1)}, bf16[1,8,4,32,8,128]{5,4,3,2,1,0:T(8,128)(2,1)}, u32[]{:S(2)}) %copy-start) | copy-done | bytes 2097176
  1.6 0.0 copy-start.1
  1.6 1.0 %copy-done.1 = bf16[1024,256]{1,0:T(8,128)(2,1)S(1)} copy-done((bf16[1024,256]{1,0:T(8,128)(2,1)S(1)}, bf16[1024,256]{1,0:T(8,128)(2,1)}, u32[]{:S(2)}) %copy-start.1) | copy-done | bytes 524312
  2.6 0.0 copy-start.2
  2.6 0.9 %copy-done.2 = bf16[256,256]{1,0:T(8,128)(2,1)S(1)} copy-done((bf16[256,256]{1,0:T(8,128)(2,1)S(1)}, bf16[256,256]{1,0:T(8,128)(2,1)}, u32[]{:S(2)}) %copy-start.2) | copy-done | bytes 131096
  3.5 0.0 copy-start.3
  3.5 0.7 %copy-done.3 = s32[512]{0:T(512)S(1)} copy-done((s32[512]{0:T(512)S(1)}, s32[512]{0:T(512)}, u32[]{:S(2)}) %copy-start.3) | copy-done | bytes 2072
  4.2 0.0 copy-start.4
  4.2 0.7 %copy-done.4 = s32[1,8]{1,0:T(1,128)S(1)} copy-done((s32[1,8]{1,0:T(1,128)S(1)}, s32[1,8]{1,0:T(1,128)}, u32[]{:S(2)}) %copy-start.4) | copy-done | bytes 56
  4.9 0.0 copy-start.5
  4.9 0.7 %copy-done.5 = f32[1,8]{1,0:T(1,128)S(1)} copy-done((f32[1,8]{1,0:T(1,128)S(1)}, f32[1,8]{1,0:T(1,128)}, u32[]{:S(2)}) %copy-start.5) | copy-done | bytes 56
  5.5 46.9 %spots.1 = bf16[8,4,256,128]{3,2,1,0:T(8,128)(2,1)S(1)} custom-call(bf16[8,4,256,128]{3,2,1,0:T(8,128)(2,1)S(1)} %bitcast.6, s32[1,8]{1,0:T(1,128)S(1)} %copy-done.4, f32[1,8]{1,0:T(1,128)S(1)} %copy-done.5, s32[512]{0:T(512)S(1)} %copy-done.3, s32[4,128]{1,0:T(4,128)S(1)} %bitcast.7, bf16[1024,256]{1,0:T(8,128)(2,1)S(1)} %copy-done.1, ...), custom_call_target="tpu_custom_call" | custom-call | tf_op jit(solution)/shard_map/spots/pallas_call | solution.py:257
  52.4 1.3 %copy.9 = bf16[8,1,1,4,32,8,128]{6,5,4,3,2,1,0:T(8,128)(2,1)} copy(bf16[8,1,1,4,32,8,128]{6,5,4,3,2,1,0:T(8,128)(2,1)S(1)} %bitcast.5) | data formatting | bytes 4194304
Async XLA Ops:
  0.0 1.6 %copy-start = (bf16[1,8,4,32,8,128]{5,4,3,2,1,0:T(8,128)(2,1)S(1)}, bf16[1,8,4,32,8,128]{5,4,3,2,1,0:T(8,128)(2,1)}, u32[]{:S(2)}) copy-start(bf16[1,8,4,32,8,128]{5,4,3,2,1,0:T(8,128)(2,1)} %param.6) | copy-start | bytes 6291460
  1.6 1.0 %copy-start.1 = (bf16[1024,256]{1,0:T(8,128)(2,1)S(1)}, bf16[1024,256]{1,0:T(8,128)(2,1)}, u32[]{:S(2)}) copy-start(bf16[1024,256]{1,0:T(8,128)(2,1)} %constant.4.clone.w1h) | copy-start | bytes 1572868
  2.6 0.9 %copy-start.2 = (bf16[256,256]{1,0:T(8,128)(2,1)S(1)}, bf16[256,256]{1,0:T(8,128)(2,1)}, u32[]{:S(2)}) copy-start(bf16[256,256]{1,0:T(8,128)(2,1)} %constant.5.clone.w2h) | copy-start | bytes 393220
  3.5 0.7 %copy-start.3 = (s32[512]{0:T(512)S(1)}, s32[512]{0:T(512)}, u32[]{:S(2)}) copy-start(s32[512]{0:T(512)} %valid.1) | copy-start | bytes 6148
  4.2 0.7 %copy-start.4 = (s32[1,8]{1,0:T(1,128)S(1)}, s32[1,8]{1,0:T(1,128)}, u32[]{:S(2)}) copy-start(s32[1,8]{1,0:T(1,128)} %shifts.1) | copy-start | bytes 100
  4.9 0.7 %copy-start.5 = (f32[1,8]{1,0:T(1,128)S(1)}, f32[1,8]{1,0:T(1,128)}, u32[]{:S(2)}) copy-start(f32[1,8]{1,0:T(1,128)} %fractions.1) | copy-start | bytes 100

commit v2 on v1

--- a/solution.py
+++ b/solution.py
@@ -52,8 +52,8 @@
     return jnp.dot(a, b, preferred_element_type=F32)
 
 
-def kernel(sizes, img, shifts, fractions, valid, counts, w1h, w2h, out, ext, send, recv, halo_out, halo_in,
-           w1, w2, diff, shifted, yhi, ylo, acc, tile_a, tile_b, tile_c, recv_a, recv_b, recv_c, inv,
+def kernel(sizes, img, shifts_h, fractions_h, valid_h, counts_h, w1h, w2h, out, shifts, fractions, valid, counts, ext, send, recv, halo_out, halo_in,
+           w1, w2, diff, shifted, yhi, ylo, acc, row_a, row_b, recv_a, recv_b, inv,
            load_sem, w_sem, send_sem, recv_sem, halo_ssem, halo_rsem, red_ssem, red_rsem):
     rounds, bricks, zs, ys, voxels = sizes
     channels, area, width = ext.shape[1:]
@@ -62,25 +62,22 @@
     z = lax.rem(col, zs)
     y = col // zs
 
-    def z_peer(d):
-        return y * zs + lax.rem(z + d, zs)
-
-    def y_peer(d):
-        return lax.rem(y + d, ys) * zs + z
-
     last = lax.axis_size("brick")
     right, left = lax.rem(col + 1, last), lax.rem(col + last - 1, last)
 
-    barrier = pltpu.get_barrier_semaphore()
-    for d in range(1, rounds):
-        pl.semaphore_signal(barrier, inc=1, device_id={"round": lax.rem(me + d, rounds)}, device_id_type=MESH)
-    for j in [right, left] + [z_peer(d) for d in range(1, zs)] + [y_peer(d) for d in range(1, ys)]:
-        pl.semaphore_signal(barrier, inc=1, device_id={"brick": j}, device_id_type=MESH)
-
     loads = [pltpu.make_async_copy(img.at[k], ext.at[k + 1], load_sem.at[k]) for k in range(bricks)]
-    loads += [pltpu.make_async_copy(w1h, w1, w_sem.at[0]), pltpu.make_async_copy(w2h, w2, w_sem.at[1])]
+    small = ((shifts_h, shifts), (fractions_h, fractions), (valid_h, valid), (w1h, w1), (w2h, w2), (counts_h, counts))
+    loads = [pltpu.make_async_copy(a, b, w_sem.at[i]) for i, (a, b) in enumerate(small)] + loads
     for c in loads:
         c.start()
+
+    line = [{"brick": y * zs + lax.rem(z + d, zs)} for d in range(1, zs)]
+    plane = [
+        {"round": lax.rem(me + a, rounds), "brick": lax.rem(y + b, ys) * zs + z}
+        for b in range(ys) for a in range(rounds) if a or b]
+    barrier = pltpu.get_barrier_semaphore()
+    for peer in [{"brick": right}, {"brick": left}] + line + plane:
+        pl.semaphore_signal(barrier, inc=1, device_id=peer, device_id_type=MESH)
 
     shape = (width, 2 * width)
     lane = iota(shape, 1)
@@ -98,7 +95,7 @@
 
     halo_out[0] = dot(flat(bricks), pack_mask((channels * width, width), 1, 0, width - HALO)).astype(BF16)
     halo_out[1] = dot(flat(1), pack_mask((channels * width, width), 1, 0, 0)).astype(BF16)
-    pl.semaphore_wait(barrier, rounds - 1 + 2 + zs - 1 + ys - 1)
+    pl.semaphore_wait(barrier, 2 + len(line) + len(plane))
 
     halos = [
         pltpu.make_async_remote_copy(
@@ -182,36 +179,27 @@
     lax.fori_loop(0, rounds, step_body, 0)
     recv[me] = send[me]
 
-    def gather(tile, slots, peers, index):
-        copies = [
+    def spread(row, slots, slot_of, peers, index):
+        for d, peer in enumerate(peers):
             pltpu.make_async_remote_copy(
-                src_ref=tile, dst_ref=slots.at[d], send_sem=red_ssem.at[index], recv_sem=red_rsem.at[index],
-                device_id=peer, device_id_type=MESH)
-            for d, peer in enumerate(peers)
-        ]
-        for c in copies:
-            c.start()
-        pltpu.make_async_copy(slots, slots, red_rsem.at[index]).wait()
-        return tile[...] + jnp.sum(slots[...], axis=0)
-
-    tile_a[...] = jnp.zeros_like(tile_a)
-    tile_a[:channels] = jnp.sum(acc[...], axis=1)
-    tile_b[...] = gather(tile_a, recv_a, [{"brick": z_peer(d)} for d in range(1, zs)], 0)
-    tile_c[...] = gather(tile_b, recv_b, [{"brick": y_peer(d)} for d in range(1, ys)], 1)
-    totals = [
-        pltpu.make_async_remote_copy(
-            src_ref=tile_c, dst_ref=recv_c.at[me], send_sem=red_ssem.at[2], recv_sem=red_rsem.at[2],
-            device_id={"round": lax.rem(me + d, rounds)}, device_id_type=MESH)
-        for d in range(1, rounds)
-    ]
-    for c in totals:
-        c.start()
-    seven = recv_c.at[pl.ds(0, rounds - 1)]
-    pltpu.make_async_copy(seven, seven, red_rsem.at[2]).wait()
-    recv_c[me] = tile_c[...]
+                src_ref=row, dst_ref=slots.at[pl.ds(slot_of(d), 1)], send_sem=red_ssem.at[index],
+                recv_sem=red_rsem.at[index], device_id=peer, device_id_type=MESH).start()
+        every = slots.at[pl.ds(0, len(peers))]
+        pltpu.make_async_copy(every, every, red_rsem.at[index]).wait()
+
+    sums = jnp.sum(jnp.sum(acc[...], axis=1), axis=1, keepdims=True)
+    group = iota((1, width), 1) // (width // channels)
+    row_a[...] = sum(jnp.where(group == c, sums[c:c + 1], 0.0) for c in range(channels))
+    spread(row_a, recv_a, lambda d: d, line, 0)
+    row_b[...] = row_a[...] + jnp.sum(recv_a[:len(line)], axis=0, keepdims=True)
+    spread(row_b, recv_b, lambda d: (d + 1) // rounds * rounds + me, plane, 1)
+    recv_b[pl.ds(me, 1)] = row_b[...]
     count = jnp.maximum(jnp.sum(counts[...].astype(F32)), 1.0)
-    total = jnp.sum(recv_c[...], axis=2, keepdims=True)
-    inv[...] = jnp.broadcast_to(1.0 / (total / (count * voxels) + 1e-06), inv.shape)
+    total = jnp.sum(recv_b[...].reshape(ys, rounds, width), axis=0)
+    scale = 1.0 / (total / (count * voxels) + 1e-06)
+    for c in range(channels):
+        lane = c * (width // channels)
+        inv[c] = jnp.broadcast_to(scale[:, lane:lane + 1], (rounds, width))
 
     for d in range(1, rounds):
         source = lax.rem(me + d, rounds)
@@ -222,12 +210,12 @@
         energy = jnp.zeros((16, width), F32)
         for r in range(rounds):
             for c in range(channels):
-                a = recv[r, c, rows].astype(F32) * inv[r, c:c + 1]
+                a = recv[r, c, rows].astype(F32) * inv[c, r:r + 1]
                 energy += a * a
         root = lax.rsqrt(energy * (1.0 / (rounds * channels)) + 1.0)
         for r in range(rounds):
             for c in range(channels):
-                a = recv[r, c, rows].astype(F32) * inv[r, c:c + 1]
+                a = recv[r, c, rows].astype(F32) * inv[c, r:r + 1]
                 out[r, c, rows] = (a * root).astype(BF16)
         return 0
 
@@ -238,9 +226,9 @@
     for d in range(1, rounds):
         k = lax.rem(me + d, rounds)
         bulk(k).wait_send()
-    pltpu.make_async_copy(recv_a, recv_a, red_ssem.at[0]).wait()
-    pltpu.make_async_copy(recv_b, recv_b, red_ssem.at[1]).wait()
-    pltpu.make_async_copy(seven, seven, red_ssem.at[2]).wait()
+    for index, (slots, peers) in enumerate(((recv_a, line), (recv_b, plane))):
+        every = slots.at[pl.ds(0, len(peers))]
+        pltpu.make_async_copy(every, every, red_ssem.at[index]).wait()
 
 
 def on_device(image, shifts, fractions, valid):
@@ -249,17 +237,20 @@
     zs, ys = 16, 4
     area = depth * height
     w1, w2 = weights(depth, height, width)
-    anywhere = pl.BlockSpec(memory_space=pl.ANY)
-    scalars = pl.BlockSpec(memory_space=pltpu.SMEM)
+    remote = pl.BlockSpec(memory_space=pltpu.HBM)
     vector = pl.BlockSpec(memory_space=pltpu.VMEM)
     tile = (8, width)
     sems = pltpu.SemaphoreType.DMA
     out = pl.pallas_call(
         functools.partial(kernel, (rounds, bricks, zs, ys, depth * height * width)),
         out_shape=jax.ShapeDtypeStruct((rounds, channels, area, width), BF16),
-        in_specs=[anywhere, scalars, scalars, scalars, vector, anywhere, anywhere],
+        in_specs=[remote] * 7,
         out_specs=vector,
         scratch_shapes=[
+            pltpu.SMEM(shifts.shape, jnp.int32),
+            pltpu.SMEM(fractions.shape, F32),
+            pltpu.SMEM(valid.shape, jnp.int32),
+            pltpu.VMEM((valid.size // width, width), jnp.int32),
             pltpu.VMEM((bricks + 2, channels, area, width), BF16),
             pltpu.VMEM((bricks, channels, area, width), BF16),
             pltpu.VMEM((rounds, channels, area, width), BF16),
@@ -272,21 +263,20 @@
             pltpu.VMEM((channels * area, 2 * width), BF16),
             pltpu.VMEM((channels * area, 2 * width), BF16),
             pltpu.VMEM((channels,) + tile, F32),
-            pltpu.VMEM(tile, F32),
-            pltpu.VMEM(tile, F32),
-            pltpu.VMEM(tile, F32),
-            pltpu.VMEM((zs - 1,) + tile, F32),
-            pltpu.VMEM((ys - 1,) + tile, F32),
-            pltpu.VMEM((rounds,) + tile, F32),
-            pltpu.VMEM((rounds,) + tile, F32),
-            sems((bricks,)), sems((2,)), sems((bricks,)), sems((rounds,)), sems((2,)), sems((2,)), sems((3,)),
-            sems((3,)),
+            pltpu.VMEM((1, width), F32),
+            pltpu.VMEM((1, width), F32),
+            pltpu.VMEM((zs, width), F32),
+            pltpu.VMEM((ys * rounds, width), F32),
+            pltpu.VMEM((channels, rounds, width), F32),
+            sems((bricks,)), sems((6,)), sems((bricks,)), sems((rounds,)), sems((2,)), sems((2,)), sems((2,)),
+            sems((2,)),
         ],
         compiler_params=pltpu.CompilerParams(
             collective_id=0, has_side_effects=True, vmem_limit_bytes=48 * 2**20),
         name="spots",
-    )(image.reshape(bricks, channels, area, width), shifts, fractions, valid, valid.reshape(-1, width),
-      jnp.asarray(w1), jnp.asarray(w2))
+    )(*[pltpu.with_memory_space_constraint(a, pltpu.HBM) for a in (
+        image.reshape(bricks, channels, area, width), shifts, fractions, valid, valid.reshape(-1, width),
+        jnp.asarray(w1), jnp.asarray(w2))])
     return out.reshape(rounds, 1, 1, channels, depth, height, width)
 
 

time: 54 us -> 49.9 us (0.924)
  local copies, waits for them, and re-layouts: 6.85 us -> 1.32 us
  Pallas kernels: 46.9 us -> 48.5 us
    unnamed x13 -> x1, local copies, waits for them, and re-layouts: 6.85 us -> 1.32 us
    pallas_call x1, Pallas kernels: 46.9 us -> 48.5 us  [on_device(): pl.pallas_call(functools.partial(kernel, (rounds, bricks, zs, ys, depth *...]
where the time goes in v2:
time: 49.9 us; the launch traced here: 49.8 us
  Pallas kernels  48.5 us (97%)
  local copies, waits for them, and re-layouts  1.32 us (3%)
    pallas_call x1, Pallas kernels, on_device(): pl.pallas_call(functools.partial(kernel, (rounds, bricks, zs, ys, depth *...  48.5 us
    unnamed x1, local copies, waits for them, and re-layouts  1.32 us

profile of v2, /device:TPU:1, one launch (start us, length us, event | category | flops | bytes accessed | tf_op | source)
XLA Modules:
  0.0 49.8 jit_solution(10200620388807641817)
XLA Ops:
  0.0 48.5 %spots.1 = bf16[8,4,256,128]{3,2,1,0:T(8,128)(2,1)S(1)} custom-call(bf16[8,4,256,128]{3,2,1,0:T(8,128)(2,1)} %bitcast.6, s32[1,8]{1,0:T(1,128)} %shifts_h.1, f32[1,8]{1,0:T(1,128)} %fractions_h.1, s32[512]{0:T(512)} %valid_h.1, s32[4,128]{1,0:T(4,128)} %bitcast.7, bf16[1024,256]{1,0:T(8,128)(2,1)} %constant.4.clone.w1h, bf16[256,256]{1,0:T(8,128)(2,1)} %constant.5.clone.w2h), custom_call_target="tpu_custom_call" | custom-call | tf_op jit(solution)/shard_map/spots/pallas_call | solution.py:244
  48.5 1.3 %copy.9 = bf16[8,1,1,4,32,8,128]{6,5,4,3,2,1,0:T(8,128)(2,1)} copy(bf16[8,1,1,4,32,8,128]{6,5,4,3,2,1,0:T(8,128)(2,1)S(1)} %bitcast.5) | data formatting | bytes 4194304

commit v3 on v2

--- a/solution.py
+++ b/solution.py
@@ -125,10 +125,13 @@
         far = 2 * there + jnp.where(late == 0, first, 1 - first)
         return jnp.where(step < 6, far, jnp.where(step == 6, 2 * chip + 1 - core, me))
 
-    def bulk(k):
+    groups = ((0, area // 2), (area // 2, area // 4), (3 * area // 4, area // 4))
+
+    def bulk(k, g):
+        rows = pl.ds(*groups[g])
         return pltpu.make_async_remote_copy(
-            src_ref=send.at[k], dst_ref=recv.at[me], send_sem=send_sem.at[k], recv_sem=recv_sem.at[me],
-            device_id={"round": k}, device_id_type=MESH)
+            src_ref=send.at[k, :, rows], dst_ref=recv.at[me, :, rows], send_sem=send_sem.at[k, g],
+            recv_sem=recv_sem.at[me, g], device_id={"round": k}, device_id_type=MESH)
 
     def filter_brick(k):
         s = shifts[0, k]
@@ -172,18 +175,19 @@
 
         @pl.when(step < rounds - 1)
         def _():
-            bulk(k).start()
+            bulk(k, 0).start()
 
         return 0
 
     lax.fori_loop(0, rounds, step_body, 0)
-    recv[me] = send[me]
 
     def spread(row, slots, slot_of, peers, index):
         for d, peer in enumerate(peers):
             pltpu.make_async_remote_copy(
                 src_ref=row, dst_ref=slots.at[pl.ds(slot_of(d), 1)], send_sem=red_ssem.at[index],
                 recv_sem=red_rsem.at[index], device_id=peer, device_id_type=MESH).start()
+
+    def arrived(slots, peers, index):
         every = slots.at[pl.ds(0, len(peers))]
         pltpu.make_async_copy(every, every, red_rsem.at[index]).wait()
 
@@ -191,8 +195,17 @@
     group = iota((1, width), 1) // (width // channels)
     row_a[...] = sum(jnp.where(group == c, sums[c:c + 1], 0.0) for c in range(channels))
     spread(row_a, recv_a, lambda d: d, line, 0)
+    later = [(step, g) for g in (1, 2) for step in [rounds - 2] + list(range(rounds - 2))]
+    held = rounds - 1 + 3
+    for step, g in later[:held]:
+        bulk(brick_of(step), g).start()
+    recv[me] = send[me]
+    arrived(recv_a, line, 0)
     row_b[...] = row_a[...] + jnp.sum(recv_a[:len(line)], axis=0, keepdims=True)
     spread(row_b, recv_b, lambda d: (d + 1) // rounds * rounds + me, plane, 1)
+    for step, g in later[held:]:
+        bulk(brick_of(step), g).start()
+    arrived(recv_b, plane, 1)
     recv_b[pl.ds(me, 1)] = row_b[...]
     count = jnp.maximum(jnp.sum(counts[...].astype(F32)), 1.0)
     total = jnp.sum(recv_b[...].reshape(ys, rounds, width), axis=0)
@@ -200,10 +213,6 @@
     for c in range(channels):
         lane = c * (width // channels)
         inv[c] = jnp.broadcast_to(scale[:, lane:lane + 1], (rounds, width))
-
-    for d in range(1, rounds):
-        source = lax.rem(me + d, rounds)
-        pltpu.make_async_copy(recv.at[source], recv.at[source], recv_sem.at[source]).wait()
 
     def norm_body(i, _):
         rows = pl.ds(pl.multiple_of(i * 16, 16), 16)
@@ -219,13 +228,19 @@
                 out[r, c, rows] = (a * root).astype(BF16)
         return 0
 
-    lax.fori_loop(0, area // 16, norm_body, 0)
+    for g, (start, size) in enumerate(groups):
+        for d in range(1, rounds):
+            source = lax.rem(me + d, rounds)
+            piece = recv.at[source, :, pl.ds(start, size)]
+            pltpu.make_async_copy(piece, piece, recv_sem.at[source, g]).wait()
+        lax.fori_loop(start // 16, (start + size) // 16, norm_body, 0)
 
     for c in halos:
         c.wait_send()
     for d in range(1, rounds):
         k = lax.rem(me + d, rounds)
-        bulk(k).wait_send()
+        for g in range(len(groups)):
+            bulk(k, g).wait_send()
     for index, (slots, peers) in enumerate(((recv_a, line), (recv_b, plane))):
         every = slots.at[pl.ds(0, len(peers))]
         pltpu.make_async_copy(every, every, red_ssem.at[index]).wait()
@@ -268,7 +283,7 @@
             pltpu.VMEM((zs, width), F32),
             pltpu.VMEM((ys * rounds, width), F32),
             pltpu.VMEM((channels, rounds, width), F32),
-            sems((bricks,)), sems((6,)), sems((bricks,)), sems((rounds,)), sems((2,)), sems((2,)), sems((2,)),
+            sems((bricks,)), sems((6,)), sems((bricks, 3)), sems((rounds, 3)), sems((2,)), sems((2,)), sems((2,)),
             sems((2,)),
         ],
         compiler_params=pltpu.CompilerParams(

time: 49.9 us -> 47.3 us (0.948)
  Pallas kernels: 48.5 us -> 45.8 us
    pallas_call x1, Pallas kernels: 48.5 us -> 45.8 us  [on_device(): pl.pallas_call(functools.partial(kernel, (rounds, bricks, zs, ys, depth *...]
where the time goes in v3:
time: 47.3 us; the launch traced here: 47.2 us
  Pallas kernels  45.8 us (97%)
  local copies, waits for them, and re-layouts  1.32 us (3%)
    pallas_call x1, Pallas kernels, on_device(): pl.pallas_call(functools.partial(kernel, (rounds, bricks, zs, ys, depth *...  45.8 us
    unnamed x1, local copies, waits for them, and re-layouts  1.32 us

profile of v3, /device:TPU:1, one launch (start us, length us, event | category | flops | bytes accessed | tf_op | source)
XLA Modules:
  0.0 47.2 jit_solution(2671093816267008824)
XLA Ops:
  0.0 45.8 %spots.1 = bf16[8,4,256,128]{3,2,1,0:T(8,128)(2,1)S(1)} custom-call(bf16[8,4,256,128]{3,2,1,0:T(8,128)(2,1)} %bitcast.6, s32[1,8]{1,0:T(1,128)} %shifts_h.1, f32[1,8]{1,0:T(1,128)} %fractions_h.1, s32[512]{0:T(512)} %valid_h.1, s32[4,128]{1,0:T(4,128)} %bitcast.7, bf16[1024,256]{1,0:T(8,128)(2,1)} %constant.4.clone.w1h, bf16[256,256]{1,0:T(8,128)(2,1)} %constant.5.clone.w2h), custom_call_target="tpu_custom_call" | custom-call | tf_op jit(solution)/shard_map/spots/pallas_call | solution.py:259
  45.9 1.3 %copy.9 = bf16[8,1,1,4,32,8,128]{6,5,4,3,2,1,0:T(8,128)(2,1)} copy(bf16[8,1,1,4,32,8,128]{6,5,4,3,2,1,0:T(8,128)(2,1)S(1)} %bitcast.5) | data formatting | bytes 4194304

commit v4 on v3

--- a/solution.py
+++ b/solution.py
@@ -54,7 +54,7 @@
 
 def kernel(sizes, img, shifts_h, fractions_h, valid_h, counts_h, w1h, w2h, out, shifts, fractions, valid, counts, ext, send, recv, halo_out, halo_in,
            w1, w2, diff, shifted, yhi, ylo, acc, row_a, row_b, recv_a, recv_b, inv,
-           load_sem, w_sem, send_sem, recv_sem, halo_ssem, halo_rsem, red_ssem, red_rsem):
+           load_sem, w_sem, send_sem, recv_sem, halo_ssem, halo_rsem, red_ssem, red_rsem, z_in, y_in):
     rounds, bricks, zs, ys, voxels = sizes
     channels, area, width = ext.shape[1:]
     me = lax.axis_index("round")
@@ -75,9 +75,21 @@
     plane = [
         {"round": lax.rem(me + a, rounds), "brick": lax.rem(y + b, ys) * zs + z}
         for b in range(ys) for a in range(rounds) if a or b]
+    def along_z(d):
+        return {"brick": y * zs + lax.rem(z + d + zs, zs)}
+
+    def along_y(d):
+        return {"brick": lax.rem(y + d + ys, ys) * zs + z}
+
+    near = [{"round": lax.rem(me + a, rounds)} for a in range(1, rounds)] + [{"brick": right}, {"brick": left}]
+    near += [along_z(1), along_z(-1), along_y(1), along_y(-1)]
+
+    def tell(sem, peers):
+        for peer in peers:
+            pl.semaphore_signal(sem, inc=1, device_id=peer, device_id_type=MESH)
+
     barrier = pltpu.get_barrier_semaphore()
-    for peer in [{"brick": right}, {"brick": left}] + line + plane:
-        pl.semaphore_signal(barrier, inc=1, device_id=peer, device_id_type=MESH)
+    tell(barrier, near)
 
     shape = (width, 2 * width)
     lane = iota(shape, 1)
@@ -95,7 +107,6 @@
 
     halo_out[0] = dot(flat(bricks), pack_mask((channels * width, width), 1, 0, width - HALO)).astype(BF16)
     halo_out[1] = dot(flat(1), pack_mask((channels * width, width), 1, 0, 0)).astype(BF16)
-    pl.semaphore_wait(barrier, 2 + len(line) + len(plane))
 
     halos = [
         pltpu.make_async_remote_copy(
@@ -103,9 +114,6 @@
             device_id={"brick": j}, device_id_type=MESH)
         for i, j in ((0, right), (1, left))
     ]
-    for c in halos:
-        c.start()
-
     def unpack_halos():
         for i, (slot, start) in enumerate(((0, width - HALO), (bricks + 1, 0))):
             halos[i].wait_recv()
@@ -173,9 +181,29 @@
         k = brick_of(step)
         filter_brick(k)
 
+        @pl.when(step == 0)
+        def _():
+            pl.semaphore_wait(barrier, len(near))
+            for c in halos:
+                c.start()
+            tell(z_in.at[0], [along_z(1), along_z(-1)])
+            tell(y_in.at[0], [along_y(1), along_y(-1)])
+
         @pl.when(step < rounds - 1)
         def _():
             bulk(k, 0).start()
+
+        @pl.when(step == 2)
+        def _():
+            pl.semaphore_wait(z_in.at[0], 2)
+            tell(z_in.at[1], [along_z(2), along_z(-2)])
+            pl.semaphore_wait(y_in.at[0], 2)
+            tell(y_in.at[1], [along_y(2)])
+
+        @pl.when(step == 4)
+        def _():
+            pl.semaphore_wait(z_in.at[1], 2)
+            tell(z_in.at[2], [along_z(4), along_z(-4)])
 
         return 0
 
@@ -194,6 +222,7 @@
     sums = jnp.sum(jnp.sum(acc[...], axis=1), axis=1, keepdims=True)
     group = iota((1, width), 1) // (width // channels)
     row_a[...] = sum(jnp.where(group == c, sums[c:c + 1], 0.0) for c in range(channels))
+    pl.semaphore_wait(z_in.at[2], 2)
     spread(row_a, recv_a, lambda d: d, line, 0)
     later = [(step, g) for g in (1, 2) for step in [rounds - 2] + list(range(rounds - 2))]
     held = rounds - 1 + 3
@@ -202,6 +231,7 @@
     recv[me] = send[me]
     arrived(recv_a, line, 0)
     row_b[...] = row_a[...] + jnp.sum(recv_a[:len(line)], axis=0, keepdims=True)
+    pl.semaphore_wait(y_in.at[1], 1)
     spread(row_b, recv_b, lambda d: (d + 1) // rounds * rounds + me, plane, 1)
     for step, g in later[held:]:
         bulk(brick_of(step), g).start()
@@ -284,7 +314,7 @@
             pltpu.VMEM((ys * rounds, width), F32),
             pltpu.VMEM((channels, rounds, width), F32),
             sems((bricks,)), sems((6,)), sems((bricks, 3)), sems((rounds, 3)), sems((2,)), sems((2,)), sems((2,)),
-            sems((2,)),
+            sems((2,)), pltpu.SemaphoreType.REGULAR((3,)), pltpu.SemaphoreType.REGULAR((2,)),
         ],
         compiler_params=pltpu.CompilerParams(
             collective_id=0, has_side_effects=True, vmem_limit_bytes=48 * 2**20),

time: 47.3 us -> 43.7 us (0.924)
  Pallas kernels: 45.8 us -> 42.2 us
    pallas_call x1, Pallas kernels: 45.8 us -> 42.2 us  [on_device(): pl.pallas_call(functools.partial(kernel, (rounds, bricks, zs, ys, depth *...]
where the time goes in v4:
time: 43.7 us; the launch traced here: 43.6 us
  Pallas kernels  42.2 us (97%)
  local copies, waits for them, and re-layouts  1.32 us (3%)
    pallas_call x1, Pallas kernels, on_device(): pl.pallas_call(functools.partial(kernel, (rounds, bricks, zs, ys, depth *...  42.2 us
    unnamed x1, local copies, waits for them, and re-layouts  1.32 us

profile of v4, /device:TPU:1, one launch (start us, length us, event | category | flops | bytes accessed | tf_op | source)
XLA Modules:
  0.0 43.6 jit_solution(10687720223316625147)
XLA Ops:
  0.0 42.2 %spots.1 = bf16[8,4,256,128]{3,2,1,0:T(8,128)(2,1)S(1)} custom-call(bf16[8,4,256,128]{3,2,1,0:T(8,128)(2,1)} %bitcast.6, s32[1,8]{1,0:T(1,128)} %shifts_h.1, f32[1,8]{1,0:T(1,128)} %fractions_h.1, s32[512]{0:T(512)} %valid_h.1, s32[4,128]{1,0:T(4,128)} %bitcast.7, bf16[1024,256]{1,0:T(8,128)(2,1)} %constant.4.clone.w1h, bf16[256,256]{1,0:T(8,128)(2,1)} %constant.5.clone.w2h), custom_call_target="tpu_custom_call" | custom-call | tf_op jit(solution)/shard_map/spots/pallas_call | solution.py:289
  42.2 1.3 %copy.9 = bf16[8,1,1,4,32,8,128]{6,5,4,3,2,1,0:T(8,128)(2,1)} copy(bf16[8,1,1,4,32,8,128]{6,5,4,3,2,1,0:T(8,128)(2,1)S(1)} %bitcast.5) | data formatting | bytes 4194304

commit v5 on v4

--- a/solution.py
+++ b/solution.py
@@ -53,7 +53,7 @@
 
 
 def kernel(sizes, img, shifts_h, fractions_h, valid_h, counts_h, w1h, w2h, out, shifts, fractions, valid, counts, ext, send, recv, halo_out, halo_in,
-           w1, w2, diff, shifted, yhi, ylo, acc, row_a, row_b, recv_a, recv_b, inv,
+           w1, w2, shifted, yhi, ylo, acc, row_a, row_b, recv_a, recv_b, inv,
            load_sem, w_sem, send_sem, recv_sem, halo_ssem, halo_rsem, red_ssem, red_rsem, z_in, y_in):
     rounds, bricks, zs, ys, voxels = sizes
     channels, area, width = ext.shape[1:]
@@ -65,9 +65,10 @@
     last = lax.axis_size("brick")
     right, left = lax.rem(col + 1, last), lax.rem(col + last - 1, last)
 
-    loads = [pltpu.make_async_copy(img.at[k], ext.at[k + 1], load_sem.at[k]) for k in range(bricks)]
     small = ((shifts_h, shifts), (fractions_h, fractions), (valid_h, valid), (w1h, w1), (w2h, w2), (counts_h, counts))
-    loads = [pltpu.make_async_copy(a, b, w_sem.at[i]) for i, (a, b) in enumerate(small)] + loads
+    order = [0, bricks - 1] + list(range(1, bricks - 1))
+    loads = [pltpu.make_async_copy(img.at[k], ext.at[k + 1], load_sem.at[k]) for k in order]
+    loads += [pltpu.make_async_copy(a, b, w_sem.at[i]) for i, (a, b) in enumerate(small)]
     for c in loads:
         c.start()
 
@@ -75,6 +76,7 @@
     plane = [
         {"round": lax.rem(me + a, rounds), "brick": lax.rem(y + b, ys) * zs + z}
         for b in range(ys) for a in range(rounds) if a or b]
+
     def along_z(d):
         return {"brick": y * zs + lax.rem(z + d + zs, zs)}
 
@@ -91,12 +93,9 @@
     barrier = pltpu.get_barrier_semaphore()
     tell(barrier, near)
 
-    shape = (width, 2 * width)
-    lane = iota(shape, 1)
-    diff[...] = iota(shape, 0) - (lane & (width - 1)) + (lane >> 7)
     acc[...] = jnp.zeros_like(acc)
-    for c in loads:
-        c.wait()
+    loads[0].wait()
+    loads[1].wait()
 
     def pack_mask(shape, packed, long, start):
         p, q = iota(shape, packed), iota(shape, long)
@@ -108,12 +107,20 @@
     halo_out[0] = dot(flat(bricks), pack_mask((channels * width, width), 1, 0, width - HALO)).astype(BF16)
     halo_out[1] = dot(flat(1), pack_mask((channels * width, width), 1, 0, 0)).astype(BF16)
 
+    pl.semaphore_wait(barrier, len(near))
     halos = [
         pltpu.make_async_remote_copy(
             src_ref=halo_out.at[i], dst_ref=halo_in.at[i], send_sem=halo_ssem.at[i], recv_sem=halo_rsem.at[i],
             device_id={"brick": j}, device_id_type=MESH)
         for i, j in ((0, right), (1, left))
     ]
+    for c in halos:
+        c.start()
+    tell(z_in.at[0], [along_z(1), along_z(-1)])
+    tell(y_in.at[0], [along_y(1), along_y(-1)])
+    for c in loads[2:]:
+        c.wait()
+
     def unpack_halos():
         for i, (slot, start) in enumerate(((0, width - HALO), (bricks + 1, 0))):
             halos[i].wait_recv()
@@ -149,29 +156,41 @@
         v_right = jnp.where(here < last * bricks - 1, valid[jnp.minimum(here + 1, last * bricks - 1)], 0)
         v_here = valid[here].astype(F32)
         v_next = jnp.where(s >= 0, v_left, v_right).astype(F32)
-        t_next = jnp.where(s >= 0, width, -width) - s
-        pick = jnp.concatenate([
-            jnp.where(diff[...] == -s, v_here, 0.0).astype(BF16),
-            jnp.where(diff[...] == t_next, v_next, 0.0).astype(BF16)], axis=0)
-        flat_rows = (channels * area, width)
-        is_left = jnp.where(s >= 0, 1.0, 0.0).astype(BF16)
-        is_right = jnp.where(s >= 0, 0.0, 1.0).astype(BF16)
-        beside = ext[k].reshape(flat_rows) * is_left + ext[k + 2].reshape(flat_rows) * is_right
-        moved = dot(jnp.concatenate([ext[k + 1].reshape(flat_rows), beside], axis=1), pick)
-        shifted[...] = ((1.0 - f) * moved[:, :width] + f * moved[:, width:]).astype(BF16)
-        field = jnp.concatenate([shifted[c * area:(c + 1) * area] for c in range(channels)], axis=1)
-        planes = dot(w1[:2 * area], field) + dot(w1[2 * area:], field)
+        ahead = s >= 0
+        turn = jnp.where(ahead, width - s, -s)
+        v_low, v_high = jnp.where(ahead, v_here, v_next), jnp.where(ahead, v_next, v_here)
+        lane = iota((1, width), 1)
+        here_part = (1.0 - f) * jnp.where(lane >= turn, v_high, v_low)
+        back_part = f * jnp.where(jnp.where(lane == 0, width, lane) >= turn, v_high, v_low)
+        lane = iota((area, width), 1)
+        is_left = jnp.where(ahead, 1.0, 0.0).astype(BF16)
+        is_right = jnp.where(ahead, 0.0, 1.0).astype(BF16)
         for c in range(channels):
-            both = jnp.concatenate([
-                planes[:area, c * width:(c + 1) * width], planes[area:, c * width:(c + 1) * width]], axis=1)
-            high = both.astype(BF16)
-            yhi[c * area:(c + 1) * area] = high
-            ylo[c * area:(c + 1) * area] = (both - high.astype(F32)).astype(BF16)
-        twice = dot(yhi[...], w2[...])
-        result = (twice[:, :width] + twice[:, width:] + dot(ylo[...], w2[:, :width])).astype(BF16)
-        send[k] = result.reshape(channels, area, width)
-        size = jnp.abs(result.astype(F32)).reshape(channels, area // 8, 8, width)
-        acc[...] += jnp.sum(size, axis=1) * v_here
+            beside = ext[k, c] * is_left + ext[k + 2, c] * is_right
+            low, high = jnp.where(ahead, ext[k + 1, c], beside), jnp.where(ahead, beside, ext[k + 1, c])
+            at = jnp.where(lane >= turn, high, low).astype(F32)
+            back = pltpu.roll(jnp.where(lane + 1 >= turn, high, low).astype(F32), 1, 1)
+            mixed = at * here_part + back * back_part
+            shifted[c * area:(c + 1) * area] = pltpu.roll(mixed, lax.rem(s + width, width), 1).astype(BF16)
+        for first in range(0, channels, 2):
+            field = jnp.concatenate([shifted[c * area:(c + 1) * area] for c in (first, first + 1)], axis=1)
+            for part in range(2):
+                planes = dot(w1[part * area:(part + 1) * area], field)
+                planes += dot(w1[(2 + part) * area:(3 + part) * area], field)
+                high = planes.astype(BF16)
+                low = (planes - high.astype(F32)).astype(BF16)
+                columns = slice(part * width, (part + 1) * width)
+                for q in range(2):
+                    rows = slice((first + q) * area, (first + q + 1) * area)
+                    yhi[rows, columns] = high[:, q * width:(q + 1) * width]
+                    ylo[rows, columns] = low[:, q * width:(q + 1) * width]
+        for c in range(channels):
+            rows = slice(c * area, (c + 1) * area)
+            twice = dot(yhi[rows], w2[...])
+            result = (twice[:, :width] + twice[:, width:] + dot(ylo[rows], w2[:, :width])).astype(BF16)
+            send[k, c] = result
+            size = jnp.abs(result.astype(F32)).reshape(area // 8, 8, width)
+            acc[c] += jnp.sum(size, axis=0) * v_here
 
     def step_body(step, _):
         @pl.when(step == 3)
@@ -180,14 +199,6 @@
 
         k = brick_of(step)
         filter_brick(k)
-
-        @pl.when(step == 0)
-        def _():
-            pl.semaphore_wait(barrier, len(near))
-            for c in halos:
-                c.start()
-            tell(z_in.at[0], [along_z(1), along_z(-1)])
-            tell(y_in.at[0], [along_y(1), along_y(-1)])
 
         @pl.when(step < rounds - 1)
         def _():
@@ -225,7 +236,7 @@
     pl.semaphore_wait(z_in.at[2], 2)
     spread(row_a, recv_a, lambda d: d, line, 0)
     later = [(step, g) for g in (1, 2) for step in [rounds - 2] + list(range(rounds - 2))]
-    held = rounds - 1 + 3
+    held = 5
     for step, g in later[:held]:
         bulk(brick_of(step), g).start()
     recv[me] = send[me]
@@ -303,7 +314,6 @@
             pltpu.VMEM((2, area, width), BF16),
             pltpu.VMEM(w1.shape, BF16),
             pltpu.VMEM(w2.shape, BF16),
-            pltpu.VMEM((width, 2 * width), jnp.int32),
             pltpu.VMEM((channels * area, width), BF16),
             pltpu.VMEM((channels * area, 2 * width), BF16),
             pltpu.VMEM((channels * area, 2 * width), BF16),

time: 43.7 us -> 42.2 us (0.966); the launches traced: 43.6 us -> 41.5 us
  Pallas kernels: 42.2 us -> 40.2 us
    pallas_call x1, Pallas kernels: 42.2 us -> 40.2 us  [on_device(): pl.pallas_call(functools.partial(kernel, (rounds, bricks, zs, ys, depth *...]
where the time goes in v5:
time: 42.2 us; the launch traced here: 41.5 us
  Pallas kernels  40.2 us (95%)
  local copies, waits for them, and re-layouts  1.32 us (3%)
    pallas_call x1, Pallas kernels, on_device(): pl.pallas_call(functools.partial(kernel, (rounds, bricks, zs, ys, depth *...  40.2 us
    unnamed x1, local copies, waits for them, and re-layouts  1.32 us

profile of v5, /device:TPU:1, one launch (start us, length us, event | category | flops | bytes accessed | tf_op | source)
XLA Modules:
  0.0 41.5 jit_solution(12393922701170455701)
XLA Ops:
  0.0 40.2 %spots.1 = bf16[8,4,256,128]{3,2,1,0:T(8,128)(2,1)S(1)} custom-call(bf16[8,4,256,128]{3,2,1,0:T(8,128)(2,1)} %bitcast.6, s32[1,8]{1,0:T(1,128)} %shifts_h.1, f32[1,8]{1,0:T(1,128)} %fractions_h.1, s32[512]{0:T(512)} %valid_h.1, s32[4,128]{1,0:T(4,128)} %bitcast.7, bf16[1024,256]{1,0:T(8,128)(2,1)} %constant.4.clone.w1h, bf16[256,256]{1,0:T(8,128)(2,1)} %constant.5.clone.w2h), custom_call_target="tpu_custom_call" | custom-call | tf_op jit(solution)/shard_map/spots/pallas_call | solution.py:300
  40.2 1.3 %copy.9 = bf16[8,1,1,4,32,8,128]{6,5,4,3,2,1,0:T(8,128)(2,1)} copy(bf16[8,1,1,4,32,8,128]{6,5,4,3,2,1,0:T(8,128)(2,1)S(1)} %bitcast.5) | data formatting | bytes 4194304

commit v6 on v5

--- a/solution.py
+++ b/solution.py
@@ -53,7 +53,7 @@
 
 
 def kernel(sizes, img, shifts_h, fractions_h, valid_h, counts_h, w1h, w2h, out, shifts, fractions, valid, counts, ext, send, recv, halo_out, halo_in,
-           w1, w2, shifted, yhi, ylo, acc, row_a, row_b, recv_a, recv_b, inv,
+           w1, w2, masks, shifted, yhi, ylo, acc, row_a, row_b, recv_a, recv_b, inv,
            load_sem, w_sem, send_sem, recv_sem, halo_ssem, halo_rsem, red_ssem, red_rsem, z_in, y_in):
     rounds, bricks, zs, ys, voxels = sizes
     channels, area, width = ext.shape[1:]
@@ -94,37 +94,31 @@
     tell(barrier, near)
 
     acc[...] = jnp.zeros_like(acc)
-    loads[0].wait()
-    loads[1].wait()
-
-    def pack_mask(shape, packed, long, start):
-        p, q = iota(shape, packed), iota(shape, long)
-        return jnp.where((p >> 5) * width + start + (p & (HALO - 1)) == q, 1.0, 0.0).astype(BF16)
-
-    def flat(k):
-        return jnp.concatenate([ext[k, c] for c in range(channels)], axis=1)
-
-    halo_out[0] = dot(flat(bricks), pack_mask((channels * width, width), 1, 0, width - HALO)).astype(BF16)
-    halo_out[1] = dot(flat(1), pack_mask((channels * width, width), 1, 0, 0)).astype(BF16)
-
-    pl.semaphore_wait(barrier, len(near))
+    long, packed = iota(masks.shape[1:], 0), iota(masks.shape[1:], 1)
+    for i, start in enumerate((width - HALO, 0)):
+        place = (packed >> 5) * width + start + (packed & (HALO - 1))
+        masks[i] = jnp.where(place == long, 1.0, 0.0).astype(BF16)
+    for c in loads:
+        c.wait()
+
     halos = [
         pltpu.make_async_remote_copy(
             src_ref=halo_out.at[i], dst_ref=halo_in.at[i], send_sem=halo_ssem.at[i], recv_sem=halo_rsem.at[i],
             device_id={"brick": j}, device_id_type=MESH)
         for i, j in ((0, right), (1, left))
     ]
-    for c in halos:
-        c.start()
-    tell(z_in.at[0], [along_z(1), along_z(-1)])
-    tell(y_in.at[0], [along_y(1), along_y(-1)])
-    for c in loads[2:]:
-        c.wait()
+
+    def send_halos():
+        for i, slot in enumerate((bricks, 1)):
+            strip = jnp.concatenate([ext[slot, c] for c in range(channels)], axis=1)
+            halo_out[i] = dot(strip, masks[i]).astype(BF16)
+            halos[i].start()
 
     def unpack_halos():
-        for i, (slot, start) in enumerate(((0, width - HALO), (bricks + 1, 0))):
+        for i, slot in enumerate((0, bricks + 1)):
             halos[i].wait_recv()
-            wide = dot(halo_in[i], pack_mask((width, channels * width), 0, 1, start)).astype(BF16)
+            wide = lax.dot_general(
+                halo_in[i], masks[i], (((1,), (1,)), ((), ())), preferred_element_type=F32).astype(BF16)
             for c in range(channels):
                 ext[slot, c] = wide[:, c * width:(c + 1) * width]
 
@@ -200,9 +194,19 @@
         k = brick_of(step)
         filter_brick(k)
 
+        @pl.when(step == 0)
+        def _():
+            pl.semaphore_wait(barrier, len(near))
+
         @pl.when(step < rounds - 1)
         def _():
             bulk(k, 0).start()
+
+        @pl.when(step == 0)
+        def _():
+            send_halos()
+            tell(z_in.at[0], [along_z(1), along_z(-1)])
+            tell(y_in.at[0], [along_y(1), along_y(-1)])
 
         @pl.when(step == 2)
         def _():
@@ -314,6 +318,7 @@
             pltpu.VMEM((2, area, width), BF16),
             pltpu.VMEM(w1.shape, BF16),
             pltpu.VMEM(w2.shape, BF16),
+            pltpu.VMEM((2, channels * width, width), BF16),
             pltpu.VMEM((channels * area, width), BF16),
             pltpu.VMEM((channels * area, 2 * width), BF16),
             pltpu.VMEM((channels * area, 2 * width), BF16),

time: 42.2 us -> 41.5 us (0.983)
  no operation moved by 1% of the time
where the time goes in v6:
time: 41.5 us; the launch traced here: 41.2 us
  Pallas kernels  39.9 us (96%)
  local copies, waits for them, and re-layouts  1.32 us (3%)
    pallas_call x1, Pallas kernels, on_device(): pl.pallas_call(functools.partial(kernel, (rounds, bricks, zs, ys, depth *...  39.9 us
    unnamed x1, local copies, waits for them, and re-layouts  1.32 us

profile of v6, /device:TPU:1, one launch (start us, length us, event | category | flops | bytes accessed | tf_op | source)
XLA Modules:
  0.0 41.2 jit_solution(2259262503942982826)
XLA Ops:
  0.0 39.9 %spots.1 = bf16[8,4,256,128]{3,2,1,0:T(8,128)(2,1)S(1)} custom-call(bf16[8,4,256,128]{3,2,1,0:T(8,128)(2,1)} %bitcast.6, s32[1,8]{1,0:T(1,128)} %shifts_h.1, f32[1,8]{1,0:T(1,128)} %fractions_h.1, s32[512]{0:T(512)} %valid_h.1, s32[4,128]{1,0:T(4,128)} %bitcast.7, bf16[1024,256]{1,0:T(8,128)(2,1)} %constant.4.clone.w1h, bf16[256,256]{1,0:T(8,128)(2,1)} %constant.5.clone.w2h), custom_call_target="tpu_custom_call" | custom-call | tf_op jit(solution)/shard_map/spots/pallas_call | solution.py:304
  39.9 1.3 %copy.9 = bf16[8,1,1,4,32,8,128]{6,5,4,3,2,1,0:T(8,128)(2,1)} copy(bf16[8,1,1,4,32,8,128]{6,5,4,3,2,1,0:T(8,128)(2,1)S(1)} %bitcast.5) | data formatting | bytes 4194304

commit v7 on v6

--- a/solution.py
+++ b/solution.py
@@ -69,9 +69,6 @@
     order = [0, bricks - 1] + list(range(1, bricks - 1))
     loads = [pltpu.make_async_copy(img.at[k], ext.at[k + 1], load_sem.at[k]) for k in order]
     loads += [pltpu.make_async_copy(a, b, w_sem.at[i]) for i, (a, b) in enumerate(small)]
-    for c in loads:
-        c.start()
-
     line = [{"brick": y * zs + lax.rem(z + d, zs)} for d in range(1, zs)]
     plane = [
         {"round": lax.rem(me + a, rounds), "brick": lax.rem(y + b, ys) * zs + z}
@@ -92,6 +89,9 @@
 
     barrier = pltpu.get_barrier_semaphore()
     tell(barrier, near)
+
+    for c in loads:
+        c.start()
 
     acc[...] = jnp.zeros_like(acc)
     long, packed = iota(masks.shape[1:], 0), iota(masks.shape[1:], 1)

time: 41.5 us -> 41.5 us (level)
  no operation moved by 1% of the time
where the time goes in v7:
time: 41.5 us; the launch traced here: 41.3 us
  Pallas kernels  40 us (96%)
  local copies, waits for them, and re-layouts  1.32 us (3%)
    pallas_call x1, Pallas kernels, on_device(): pl.pallas_call(functools.partial(kernel, (rounds, bricks, zs, ys, depth *...  40 us
    unnamed x1, local copies, waits for them, and re-layouts  1.32 us

profile of v7, /device:TPU:1, one launch (start us, length us, event | category | flops | bytes accessed | tf_op | source)
XLA Modules:
  0.0 41.3 jit_solution(14114367311130147211)
XLA Ops:
  0.0 40.0 %spots.1 = bf16[8,4,256,128]{3,2,1,0:T(8,128)(2,1)S(1)} custom-call(bf16[8,4,256,128]{3,2,1,0:T(8,128)(2,1)} %bitcast.6, s32[1,8]{1,0:T(1,128)} %shifts_h.1, f32[1,8]{1,0:T(1,128)} %fractions_h.1, s32[512]{0:T(512)} %valid_h.1, s32[4,128]{1,0:T(4,128)} %bitcast.7, bf16[1024,256]{1,0:T(8,128)(2,1)} %constant.4.clone.w1h, bf16[256,256]{1,0:T(8,128)(2,1)} %constant.5.clone.w2h), custom_call_target="tpu_custom_call" | custom-call | tf_op jit(solution)/shard_map/spots/pallas_call | solution.py:304
  40.0 1.3 %copy.9 = bf16[8,1,1,4,32,8,128]{6,5,4,3,2,1,0:T(8,128)(2,1)} copy(bf16[8,1,1,4,32,8,128]{6,5,4,3,2,1,0:T(8,128)(2,1)S(1)} %bitcast.5) | data formatting | bytes 4194304
